TPU v7x, 512 devices: a whole 4x8x8 slice. The times are simulated.
512 devices in a mesh: pipe: 32 (over y_hi, z), tensor: 8 (over y_lo, x), dp: 2 (over core).
Axes of the slice: x: 4, y: 8 (y_hi: 4, y_lo: 2; y = y_hi * 2 + y_lo), z: 8, core: 2. Of those that a mesh axis runs over, the one named last changes fastest.
Arguments:
- fwd_in: bfloat16 [32, 512, 4096], P('pipe', 'dp', 'tensor'), may hold values from -6 to 6
- parked: bfloat16 [32, 512, 4096], P('pipe', 'dp', 'tensor'), may hold values from -6 to 6
- grad_in: bfloat16 [32, 512, 4096], P('pipe', 'dp', 'tensor'), may hold values from -6 to 6
- positions: int32 [32, 2, 2], P('pipe', 'dp'), may hold values from 0 to 768, as said below
- kv_cache: bfloat16 [32, 2, 2, 512, 256], P('pipe', 'dp'), may hold values from -6 to 6
- w_query: bfloat16 [32, 4096, 1024], P('pipe', 'tensor', 'dp'), may hold values from -0.09375 to 0.09375
- w_keyval: bfloat16 [32, 4096, 256], P('pipe', 'tensor'), may hold values from -0.09375 to 0.09375
- w_out: bfloat16 [32, 1024, 4096], P('pipe', 'tensor', 'dp'), may hold values from -0.1875 to 0.1875
- gain: bfloat16 [32, 4096], P('pipe', 'tensor'), may hold values from 0.5 to 1.5
Outputs:
- next_act: bfloat16 [32, 512, 4096], P('pipe', 'dp', 'tensor')
- prev_grad: bfloat16 [32, 512, 4096], P('pipe', 'dp', 'tensor')
- grad_query: bfloat16 [32, 4096, 1024], P('pipe', 'tensor', 'dp')
- grad_keyval: float32 [32, 4096, 256], P('pipe', 'tensor')
- grad_out: bfloat16 [32, 1024, 4096], P('pipe', 'tensor', 'dp')
- grad_gain: float32 [32, 4096], P('pipe', 'tensor')
Inputs may be any that keep to these rules, and one draw needn't show every extreme that they name: `positions`: each is a multiple of 256.
All inputs are finite; a program needn't handle non-finite values.
Results may differ from a plain program's by a relative error of at most 0.028.
Values may be sent and summed in bfloat16 or wider, within the bound.
A program may use at most 64 MiB of HBM per device.

v0:
```python
import math

import jax
import jax.numpy as jnp
from jax import lax
from jax.sharding import PartitionSpec as P

HEAD = 128


eps = 1e-05


def shifted(value, axis, by):
    peers = lax.axis_size(axis)
    pairs = [(i, i + by) for i in range(peers) if 0 <= i + by < peers]
    return lax.ppermute(value, axis, pairs)


def partner(block, axis, apart):
    count = lax.axis_size(axis)
    route = []
    for low in range(count):
        high = low | 1 << apart
        if high != low and high < count:
            route += [(low, high), (high, low)]
    return lax.ppermute(block, axis, route)


def visible(rows, span, start):
    column = jnp.arange(span + rows, dtype=jnp.int32)[None, :]
    line = jnp.arange(rows, dtype=jnp.int32)[:, None]
    live = jnp.minimum(start, span)
    return jnp.where(column < span, column >= span - live, column - span <= line)


def attend(query, keyval, cache, start, heads):
    rows = query.shape[0]
    span = cache.shape[0]
    size = keyval.shape[1] // 2
    keys = jnp.concatenate([cache[:, :size], keyval[:, :size]], axis=0)
    values = jnp.concatenate([cache[:, size:], keyval[:, size:]], axis=0)
    query_heads = query.reshape(rows, heads, size)
    scores = jnp.einsum(
        "rhd,kd->hrk", query_heads, keys, preferred_element_type=jnp.float32
    ) / math.sqrt(size)
    scores = jnp.where(visible(rows, span, start)[None], scores, -1e30)
    weights = jax.nn.softmax(scores, axis=-1)
    probs = weights.astype(jnp.bfloat16)
    mixed = jnp.einsum("hrk,kd->rhd", probs, values, preferred_element_type=jnp.float32)
    return (
        mixed.reshape(rows, heads * size).astype(jnp.bfloat16),
        weights,
        probs,
        keys,
        values,
        query_heads,
    )


def attend_back(grad_mixed, weights, probs, keys, values, query_heads, span):
    rows, heads, size = query_heads.shape
    grad_heads = grad_mixed.reshape(rows, heads, size)
    grad_probs = jnp.einsum("rhd,kd->hrk", grad_heads, values, preferred_element_type=jnp.float32)
    grad_scores = (
        weights
        * (grad_probs - jnp.sum(grad_probs * weights, axis=-1, keepdims=True))
        / math.sqrt(size)
    )
    scores_low = grad_scores.astype(jnp.bfloat16)
    grad_query = jnp.einsum(
        "hrk,kd->rhd", scores_low, keys, preferred_element_type=jnp.float32
    ).reshape(rows, heads * size)
    grad_keys = jnp.einsum(
        "hrk,rhd->kd", scores_low[:, :, span:], query_heads, preferred_element_type=jnp.float32
    )
    grad_values = jnp.einsum(
        "hrk,rhd->kd", probs[:, :, span:], grad_heads, preferred_element_type=jnp.float32
    )
    return (grad_query, jnp.concatenate([grad_keys, grad_values], axis=1))


def contract(left, right, left_dim, right_dim):
    return lax.dot_general(
        left, right, (((left_dim,), (right_dim,)), ((), ())), preferred_element_type=jnp.float32
    )


def local(fwd_in, parked, grad_in, positions, kv_cache, w_query, w_keyval, w_out, gain):
    heads = w_out.shape[1] // HEAD
    width = w_query.shape[1] * lax.axis_size("tensor")
    query_full, out_full = (
        lax.all_gather(w_query[0], "dp", axis=1, tiled=True),
        lax.all_gather(w_out[0], "dp", axis=1, tiled=True),
    )
    keyval_w = w_keyval[0]
    gain_row = gain[0].astype(jnp.float32)
    span = kv_cache.shape[3]

    def prepare(x, cache, start):
        xf = x.astype(jnp.float32)
        totals = lax.psum(jnp.sum(xf * xf, axis=1), "tensor")
        scale = lax.rsqrt(totals / width + eps)
        normed = (xf * scale[:, None] * gain_row).astype(jnp.bfloat16)
        query_part = jnp.dot(normed, query_full, preferred_element_type=jnp.float32)
        keyval_part = jnp.dot(normed, keyval_w, preferred_element_type=jnp.float32)
        query_all, keyval = (
            lax.psum(query_part.astype(jnp.bfloat16), "tensor").astype(jnp.float32),
            lax.psum(keyval_part.astype(jnp.bfloat16), "tensor").astype(jnp.float32),
        )
        query = lax.dynamic_slice_in_dim(
            query_all, lax.axis_index("tensor") * heads * HEAD, heads * HEAD, 1
        )
        found = attend(query.astype(jnp.bfloat16), keyval.astype(jnp.bfloat16), cache, start, heads)
        return (xf, scale, normed, found)

    xf, scale_fwd, normed_fwd, found_fwd = prepare(fwd_in[0], kv_cache[0, 0, 0], positions[0, 0, 0])
    partial_value = jnp.dot(found_fwd[0], out_full, preferred_element_type=jnp.float32)
    added = lax.psum_scatter(
        partial_value.astype(jnp.bfloat16), "tensor", scatter_dimension=1, tiled=True
    ).astype(jnp.float32)
    result = (xf + added).astype(jnp.bfloat16)
    next_act = shifted(result, "pipe", 1)
    levels = lax.axis_size("pipe").bit_length() - 1
    order = list(range(levels))
    saved = parked[0]
    for bit in order:
        saved = partner(saved, "pipe", bit)
    saved_f, saved_scale, saved_normed, found_bwd = prepare(
        saved, kv_cache[0, 0, 1], positions[0, 0, 1]
    )
    mixed_b, weights, probs, keys, values, query_heads = found_bwd
    grad = grad_in[0]
    grad_full = lax.all_gather(grad, "tensor", axis=1, tiled=True)
    grad_wout = contract(mixed_b, grad_full, 0, 0)
    grad_mixed = contract(grad_full, out_full, 1, 1).astype(jnp.bfloat16)
    grad_q, grad_kv = attend_back(grad_mixed, weights, probs, keys, values, query_heads, span)
    query_grads = lax.all_gather(grad_q.astype(jnp.bfloat16), "tensor", axis=1, tiled=True)
    keyval_grads = lax.psum(grad_kv.astype(jnp.bfloat16), "tensor")
    grad_wq = contract(saved_normed, query_grads, 0, 0)
    grad_wkv = contract(saved_normed, keyval_grads, 0, 0)
    grad_normed = contract(query_grads, query_full, 1, 1) + contract(keyval_grads, keyval_w, 1, 1)
    grad_gain = jnp.sum(grad_normed * saved_f * saved_scale[:, None], axis=0)
    grad_x = grad.astype(jnp.float32) + grad_normed * gain_row * saved_scale[:, None]
    prev_grad = shifted(grad_x.astype(jnp.bfloat16), "pipe", -1)
    shard_query, shard_out = (
        lax.psum_scatter(
            grad_wq.astype(jnp.bfloat16), "dp", scatter_dimension=1, tiled=True
        ).astype(jnp.float32),
        lax.psum_scatter(
            grad_wout.astype(jnp.bfloat16), "dp", scatter_dimension=1, tiled=True
        ).astype(jnp.float32),
    )
    summed_kv, summed_gain = (
        lax.psum(grad_wkv.astype(jnp.bfloat16), "dp").astype(jnp.float32),
        lax.psum(grad_gain.astype(jnp.bfloat16), "dp").astype(jnp.float32),
    )
    return (
        next_act[None],
        prev_grad[None],
        shard_query.astype(jnp.bfloat16)[None],
        summed_kv[None],
        shard_out.astype(jnp.bfloat16)[None],
        summed_gain[None],
    )


def solution(mesh):
    return jax.shard_map(
        local,
        mesh=mesh,
        in_specs=(
            P("pipe", "dp", "tensor"),
            P("pipe", "dp", "tensor"),
            P("pipe", "dp", "tensor"),
            P("pipe", "dp", None),
            P("pipe", "dp", None, None, None),
            P("pipe", "tensor", "dp"),
            P("pipe", "tensor", None),
            P("pipe", "tensor", "dp"),
            P("pipe", "tensor"),
        ),
        out_specs=(
            P("pipe", "dp", "tensor"),
            P("pipe", "dp", "tensor"),
            P("pipe", "tensor", "dp"),
            P("pipe", "tensor", None),
            P("pipe", "tensor", "dp"),
            P("pipe", "tensor"),
        ),
        check_vma=False,
    )
```

profile of v0, /device:TPU:1, one launch (start us, length us, event | category | flops | bytes accessed | tf_op | source)
XLA Modules:
  0.0 500.6 jit_solution(4870465936944510648)
XLA Ops:
  7.2 5.0 collective-permute-start.1
  12.2 4.0 collective-permute-done.1
  16.2 8.1 %collective-permute-start.2 = (bf16[256,512]{1,0:T(8,128)(2,1)S(1)}, bf16[256,512]{1,0:T(8,128)(2,1)S(1)}, u32[]{:S(2)}, u32[]{:S(2)}) collective-permute-start(bf16[256,512]{1,0:T(8,128)(2,1)S(1)} %collective-permute-done.1), channel_id=1, source_target_pairs={{0,32},{32,0},{16,48},{48,16},{64,96},{96,64},{80,112},{112,80},{1... | collective-permute-start | bytes 786440 | tf_op jit(solution)/shard_map/ppermute | solution.py:27
  24.2 11.4 %collective-permute-done.2 = bf16[256,512]{1,0:T(8,128)(2,1)S(1)} collective-permute-done((bf16[256,512]{1,0:T(8,128)(2,1)S(1)}, bf16[256,512]{1,0:T(8,128)(2,1)S(1)}, u32[]{:S(2)}, u32[]{:S(2)}) %collective-permute-start.2) | collective-permute-done | bytes 262176 | tf_op jit(solution)/shard_map/ppermute | solution.py:27
  35.7 8.1 %collective-permute-start.3 = (bf16[256,512]{1,0:T(8,128)(2,1)S(1)}, bf16[256,512]{1,0:T(8,128)(2,1)S(1)}, u32[]{:S(2)}, u32[]{:S(2)}) collective-permute-start(bf16[256,512]{1,0:T(8,128)(2,1)S(1)} %collective-permute-done.2), channel_id=1, source_target_pairs={{0,64},{64,0},{16,80},{80,16},{32,96},{96,32},{48,112},{112,48},{1... | collective-permute-start | bytes 786440 | tf_op jit(solution)/shard_map/ppermute | solution.py:27
  43.8 8.0 %collective-permute-done.3 = bf16[256,512]{1,0:T(8,128)(2,1)S(1)} collective-permute-done((bf16[256,512]{1,0:T(8,128)(2,1)S(1)}, bf16[256,512]{1,0:T(8,128)(2,1)S(1)}, u32[]{:S(2)}, u32[]{:S(2)}) %collective-permute-start.3) | collective-permute-done | bytes 262176 | tf_op jit(solution)/shard_map/ppermute | solution.py:27
  51.8 4.2 collective-permute-start.4
  56.0 7.1 %collective-permute-done.4 = bf16[256,512]{1,0:T(8,128)(2,1)S(1)} collective-permute-done((bf16[256,512]{1,0:T(8,128)(2,1)S(1)}, bf16[256,512]{1,0:T(8,128)(2,1)S(1)}, u32[]{:S(2)}, u32[]{:S(2)}) %collective-permute-start.4) | collective-permute-done | bytes 262176 | tf_op jit(solution)/shard_map/ppermute | solution.py:27
  63.1 10.3 %collective-permute-start.5 = (bf16[256,512]{1,0:T(8,128)(2,1)S(1)}, bf16[256,512]{1,0:T(8,128)(2,1)S(1)}, u32[]{:S(2)}, u32[]{:S(2)}) collective-permute-start(bf16[256,512]{1,0:T(8,128)(2,1)S(1)} %collective-permute-done.4), channel_id=1, source_target_pairs={{0,256},{256,0},{16,272},{272,16},{32,288},{288,32},{48,304},{304,... | collective-permute-start | bytes 786440 | tf_op jit(solution)/shard_map/ppermute | solution.py:27
  73.4 0.7 mul.103
  74.0 1.1 fusion.27
  75.1 7.3 %collective-permute-done.5 = bf16[256,512]{1,0:T(8,128)(2,1)S(1)} collective-permute-done((bf16[256,512]{1,0:T(8,128)(2,1)S(1)}, bf16[256,512]{1,0:T(8,128)(2,1)S(1)}, u32[]{:S(2)}, u32[]{:S(2)}) %collective-permute-start.5) | collective-permute-done | bytes 262176 | tf_op jit(solution)/shard_map/ppermute | solution.py:27
  82.5 0.1 fusion.33
  82.6 13.8 %all-reduce = (f32[256]{0:T(256)S(1)}, f32[256]{0:T(256)S(1)}) all-reduce(f32[256]{0:T(256)S(1)} %fusion.27, f32[256]{0:T(256)S(1)} %fusion.33), channel_id=1, replica_groups=mesh['pipe'=32,'tensor'=8,'dp'=2] {'tensor'}, use_global_device_ids=true, to_apply=%region_1.0 | all-reduce | flops 512 | bytes 4096 | tf_op jit(solution)/shard_map/psum | solution.py:102
  96.5 2.5 convolution_convert_fusion.3
  99.0 0.9 convolution_convert_fusion.6
  100.0 0.7 all-gather.10.cloned.1.call-update
  100.7 0.5 all-gather.12.cloned.1.call-update
  101.3 0.6 fusion.91
  102.7 0.9 convolution_convert_fusion.7
  103.7 1.3 convolution_convert_fusion.4
  105.0 85.7 %all-reduce.11.cloned.1.call-done = (bf16[256,256]{1,0:T(8,128)(2,1)}, bf16[256,1024]{1,0:T(8,128)(2,1)}) async-done(((bf16[256,256]{1,0:T(8,128)(2,1)}, bf16[256,1024]{1,0:T(8,128)(2,1)}), (bf16[256,256]{1,0:T(8,128)(2,1)}, bf16[256,1024]{1,0:T(8,128)(2,1)})) %all-reduce.11.cloned.1.call-update) | async-done | bytes 655376 | tf_op jit(solution)/shard_map/psum | solution.py:109
  190.6 0.9 fusion.90
  191.5 1.3 fusion.92
  192.8 0.2 fusion.23
  193.0 23.0 %all-gather.10.cloned.1.call-done = bf16[1,128,4096]{2,1,0:T(8,128)(2,1)} async-done(((bf16[1,128,2048]{2,1,0:T(8,128)(2,1)}), bf16[1,128,4096]{2,1,0:T(8,128)(2,1)}) %all-gather.10.cloned.1.call-update) | async-done | bytes 1048592 | tf_op jit(solution)/shard_map/all_gather | solution.py:94
  216.0 43.8 %all-gather.12.cloned.1.call-done = bf16[1,256,4096]{2,1,0:T(8,128)(2,1)} async-done(((bf16[1,256,512]{2,1,0:T(8,128)(2,1)}), bf16[1,256,4096]{2,1,0:T(8,128)(2,1)}) %all-gather.12.cloned.1.call-update) | async-done | bytes 2097168 | tf_op jit(solution)/shard_map/all_gather | solution.py:134
  259.8 2.6 fusion.8
  262.4 0.3 multiply_reduce_fusion
  262.8 0.2 multiply_convert_fusion
  263.0 1.2 convolution_convert_fusion.12
  264.2 0.2 convolution_convert_fusion.11
  264.4 0.7 pad_maximum_fusion.2
  265.1 0.0 reduce-scatter.4.cloned.1.call-start
  265.8 0.6 iota_compare_fusion.2
  266.4 0.7 fusion.87
  267.1 84.2 %all-reduce.9.cloned.1.call-done = (bf16[256,256]{1,0:T(8,128)(2,1)}, bf16[256,1024]{1,0:T(8,128)(2,1)}, bf16[256,256]{0,1:T(8,128)(2,1)}) async-done(((bf16[256,256]{1,0:T(8,128)(2,1)}, bf16[256,1024]{1,0:T(8,128)(2,1)}, bf16[256,256]{0,1:T(8,128)(2,1)}), (bf16[256,256]{1,0:T(8,128)(2,1)}, bf16[256,1024]{1,0:T(8,128)(2,1)}, bf16[256,256]{0,1:T(8,128)(2,1)})) %all-reduce.9.cloned.1.call-update) | async-done | bytes 786448 | tf_op jit(solution)/shard_map/psum | solution.py:109
  351.3 1.5 fusion.89
  352.8 1.4 fusion.93
  354.2 0.2 fusion.21
  354.3 3.3 convolution_convert_fusion
  357.7 0.0 all-reduce.7.cloned.1.call-start
  357.7 0.8 copy-done.12
  358.5 0.3 fusion.12
  358.8 25.8 %all-gather.3 = bf16[256,1,1024]{0,2,1:T(8,128)(2,1)} all-gather(bf16[256,1,128]{0,2,1:T(8,128)(2,1)S(1)} %fusion.12), channel_id=5, replica_groups=mesh['pipe'=32,'tensor'=8,'dp'=2] {'tensor'}, dimensions={2}, use_global_device_ids=true | all-gather | bytes 589824 | tf_op jit(solution)/shard_map/all_gather | solution.py:138
  384.6 2.0 fusion.7
  386.7 0.0 reduce-scatter.6.cloned.1.call-start
  386.7 2.7 convolution_convert_fusion.2
  389.4 0.0 reduce-scatter.8.cloned.1.call-start
  389.5 2.8 convolution_convert_fusion.1
  392.3 0.3 fusion.51
  392.6 1.8 fusion.37
  394.4 1.3 collective-permute-start.6
  395.7 13.1 %reduce-scatter.4.cloned.1.call-done = bf16[256,512]{1,0:T(8,128)(2,1)} async-done(((bf16[256,4096]{1,0:T(8,128)(2,1)}), bf16[256,512]{1,0:T(8,128)(2,1)}) %reduce-scatter.4.cloned.1.call-update) | async-done | bytes 262160 | tf_op jit(solution)/shard_map/reduce_scatter | solution.py:119
  408.8 1.0 fusion.30
  409.8 1.3 collective-permute-start
  411.1 7.4 %psum.71 = bf16[1,512]{1,0:T(2,128)(2,1)S(1)} all-reduce(bf16[1,512]{1,0:T(2,128)(2,1)S(1)} %broadcast_in_dim.83), channel_id=1, replica_groups=mesh['pipe'=32,'tensor'=8,'dp'=2] {'dp'}, use_global_device_ids=true, to_apply=%region_19.20 | all-reduce | flops 512 | bytes 2048 | tf_op jit(solution)/shard_map/psum | solution.py:156
  418.5 0.6 broadcast_in_dim.84
  419.1 30.6 %all-reduce.7.cloned.1.call-done = bf16[1,512,256]{2,1,0:T(8,128)(2,1)} async-done(((bf16[1,512,256]{2,1,0:T(8,128)(2,1)}), bf16[1,512,256]{2,1,0:T(8,128)(2,1)}) %all-reduce.7.cloned.1.call-update) | async-done | bytes 262160 | tf_op jit(solution)/shard_map/psum | solution.py:155
  449.7 1.8 broadcast_in_dim.81
  451.5 19.6 %reduce-scatter.6.cloned.1.call-done = bf16[512,512]{1,0:T(8,128)(2,1)} async-done(((bf16[512,1024]{1,0:T(8,128)(2,1)}), bf16[512,512]{1,0:T(8,128)(2,1)}) %reduce-scatter.6.cloned.1.call-update) | async-done | bytes 524304 | tf_op jit(solution)/shard_map/reduce_scatter | solution.py:147
  471.1 21.6 %reduce-scatter.8.cloned.1.call-done = bf16[128,2048]{1,0:T(8,128)(2,1)} async-done(((bf16[128,4096]{1,0:T(8,128)(2,1)}), bf16[128,2048]{1,0:T(8,128)(2,1)}) %reduce-scatter.8.cloned.1.call-update) | async-done | bytes 524304 | tf_op jit(solution)/shard_map/reduce_scatter | solution.py:150
  492.7 0.7 copy.23
  493.4 0.7 copy.24
  (57 shorter events, 0.5 us)
Async XLA Ops:
  7.2 91.8 %copy-start = (bf16[1,512,256]{2,1,0:T(8,128)(2,1)S(1)}, bf16[1,512,256]{2,1,0:T(8,128)(2,1)}, u32[]{:S(2)}) copy-start(bf16[1,512,256]{2,1,0:T(8,128)(2,1)} %param.15) | copy-start | bytes 786436
  7.2 89.3 %all-gather.8.cloned.1.call-start = ((), (), s32[]{:S(2)}) async-start(), calls=%async_computation.7 | async-start | bytes 1572864 | tf_op jit(solution)/shard_map/all_gather | solution.py:93
  7.2 8.9 %collective-permute-start.1 = (bf16[256,512]{1,0:T(8,128)(2,1)}, bf16[256,512]{1,0:T(8,128)(2,1)S(1)}, u32[]{:S(2)}, u32[]{:S(2)}) collective-permute-start(bf16[256,512]{1,0:T(8,128)(2,1)} %bitcast.140), channel_id=1, source_target_pairs={{0,16},{16,0},{32,48},{48,32},{64,80},{80,64},{96,112},{112,96},{1... | collective-permute-start | bytes 786440 | tf_op jit(solution)/shard_map/ppermute | solution.py:27
  16.2 19.5 %collective-permute-start.2 = (bf16[256,512]{1,0:T(8,128)(2,1)S(1)}, bf16[256,512]{1,0:T(8,128)(2,1)S(1)}, u32[]{:S(2)}, u32[]{:S(2)}) collective-permute-start(bf16[256,512]{1,0:T(8,128)(2,1)S(1)} %collective-permute-done.1), channel_id=1, source_target_pairs={{0,32},{32,0},{16,48},{48,16},{64,96},{96,64},{80,112},{112,80},{1... | collective-permute-start | bytes 786440 | tf_op jit(solution)/shard_map/ppermute | solution.py:27
  35.7 16.1 %collective-permute-start.3 = (bf16[256,512]{1,0:T(8,128)(2,1)S(1)}, bf16[256,512]{1,0:T(8,128)(2,1)S(1)}, u32[]{:S(2)}, u32[]{:S(2)}) collective-permute-start(bf16[256,512]{1,0:T(8,128)(2,1)S(1)} %collective-permute-done.2), channel_id=1, source_target_pairs={{0,64},{64,0},{16,80},{80,16},{32,96},{96,32},{48,112},{112,48},{1... | collective-permute-start | bytes 786440 | tf_op jit(solution)/shard_map/ppermute | solution.py:27
  43.8 146.8 %all-reduce.11.cloned.1.call-start = ((), (), s32[]{:S(2)}) async-start(), calls=%async_computation.11 | async-start | bytes 1310720 | tf_op jit(solution)/shard_map/psum | solution.py:109
  51.8 11.3 %collective-permute-start.4 = (bf16[256,512]{1,0:T(8,128)(2,1)S(1)}, bf16[256,512]{1,0:T(8,128)(2,1)S(1)}, u32[]{:S(2)}, u32[]{:S(2)}) collective-permute-start(bf16[256,512]{1,0:T(8,128)(2,1)S(1)} %collective-permute-done.3), channel_id=1, source_target_pairs={{0,128},{128,0},{16,144},{144,16},{32,160},{160,32},{48,176},{176,... | collective-permute-start | bytes 786440 | tf_op jit(solution)/shard_map/ppermute | solution.py:27
  63.1 19.3 %collective-permute-start.5 = (bf16[256,512]{1,0:T(8,128)(2,1)S(1)}, bf16[256,512]{1,0:T(8,128)(2,1)S(1)}, u32[]{:S(2)}, u32[]{:S(2)}) collective-permute-start(bf16[256,512]{1,0:T(8,128)(2,1)S(1)} %collective-permute-done.4), channel_id=1, source_target_pairs={{0,256},{256,0},{16,272},{272,16},{32,288},{288,32},{48,304},{304,... | collective-permute-start | bytes 786440 | tf_op jit(solution)/shard_map/ppermute | solution.py:27
  82.5 16.5 %copy-start.3 = (bf16[256,512]{1,0:T(8,128)(2,1)}, bf16[256,512]{1,0:T(8,128)(2,1)S(1)}, u32[]{:S(2)}) copy-start(bf16[256,512]{1,0:T(8,128)(2,1)S(1)} %collective-permute-done.5) | copy-start | bytes 786436
  82.6 18.7 %copy-start.16 = (s32[1,1,2]{2,1,0:T(1,128)S(1)}, s32[1,1,2]{2,1,0:T(1,128)}, u32[]{:S(2)}) copy-start(s32[1,1,2]{2,1,0:T(1,128)} %param.12) | copy-start | bytes 28
  82.6 20.0 %copy-start.9 = (bf16[1,1,2,512,256]{4,3,2,1,0:T(8,128)(2,1)S(1)}, bf16[1,1,2,512,256]{4,3,2,1,0:T(8,128)(2,1)}, u32[]{:S(2)}) copy-start(bf16[1,1,2,512,256]{4,3,2,1,0:T(8,128)(2,1)} %param.13) | copy-start | bytes 1572868
  99.0 3.7 copy-start.4
  99.9 3.7 copy-start.2
  100.0 116.1 %all-gather.10.cloned.1.call-start = ((), (), s32[]{:S(2)}) async-start(), calls=%async_computation.8 | async-start | bytes 1572864 | tf_op jit(solution)/shard_map/all_gather | solution.py:94
  100.7 159.1 %all-gather.12.cloned.1.call-start = ((), (), s32[]{:S(2)}) async-start(), calls=%async_computation.9 | async-start | bytes 2359296 | tf_op jit(solution)/shard_map/all_gather | solution.py:134
  101.3 250.0 %all-reduce.9.cloned.1.call-start = ((), (), s32[]{:S(2)}) async-start(), calls=%async_computation.10 | async-start | bytes 1572864 | tf_op jit(solution)/shard_map/psum | solution.py:109
  102.6 88.9 %copy-start.17 = (pred[768]{0:T(1024)(128)(4,1)}, pred[768]{0:T(1024)(128)(4,1)S(1)}, u32[]{:S(2)}) copy-start(pred[768]{0:T(1024)(128)(4,1)S(1)} %get-tuple-element.36) | copy-start | bytes 2308
  102.7 90.1 %copy-start.11 = (bf16[512,128]{1,0:T(8,128)(2,1)}, bf16[512,128]{1,0:T(8,128)(2,1)S(1)}, u32[]{:S(2)}) copy-start(bf16[512,128]{1,0:T(8,128)(2,1)S(1)} %get-tuple-element.22) | copy-start | bytes 393220
  102.7 159.7 %copy-start.10 = (bf16[512,128]{1,0:T(8,128)(2,1)}, bf16[512,128]{1,0:T(8,128)(2,1)S(1)}, u32[]{:S(2)}) copy-start(bf16[512,128]{1,0:T(8,128)(2,1)S(1)} %get-tuple-element.21) | copy-start | bytes 393220
  191.5 70.9 %copy-start.14 = (bf16[256,128]{1,0:T(8,128)(2,1)}, bf16[256,128]{1,0:T(8,128)(2,1)S(1)}, u32[]{:S(2)}) copy-start(bf16[256,128]{1,0:T(8,128)(2,1)S(1)} %get-tuple-element.26) | copy-start | bytes 196612
  191.5 70.9 %copy-start.13 = (bf16[256,128]{1,0:T(8,128)(2,1)}, bf16[256,128]{1,0:T(8,128)(2,1)S(1)}, u32[]{:S(2)}) copy-start(bf16[256,128]{1,0:T(8,128)(2,1)S(1)} %get-tuple-element.25) | copy-start | bytes 196612
  263.0 1.2 copy-start.6
  265.1 89.3 %copy-start.7 = (bf16[1,128,4096]{2,1,0:T(8,128)(2,1)S(1)}, bf16[1,128,4096]{2,1,0:T(8,128)(2,1)}, u32[]{:S(2)}) copy-start(bf16[1,128,4096]{2,1,0:T(8,128)(2,1)} %all-gather.10.cloned.1.call-done) | copy-start | bytes 3145732
  265.1 143.7 %reduce-scatter.4.cloned.1.call-start = ((), (), s32[]{:S(2)}) async-start(), calls=%async_computation.3 | async-start | bytes 2359296 | tf_op jit(solution)/shard_map/reduce_scatter | solution.py:119
  357.6 0.9 copy-start.12
  357.6 0.9 copy-start.15
  357.6 27.0 %copy-start.8 = (bf16[256,256]{0,1:T(8,128)(2,1)S(1)}, bf16[256,256]{0,1:T(8,128)(2,1)}, u32[]{:S(2)}) copy-start(bf16[256,256]{0,1:T(8,128)(2,1)} %get-tuple-element.10) | copy-start | bytes 393220
  357.7 92.0 %all-reduce.7.cloned.1.call-start = ((), (), s32[]{:S(2)}) async-start(), calls=%async_computation.5 | async-start | bytes 524288 | tf_op jit(solution)/shard_map/psum | solution.py:155
  358.8 30.7 %copy-start.1 = (bf16[1,256,4096]{2,1,0:T(8,128)(2,1)S(1)}, bf16[1,256,4096]{2,1,0:T(8,128)(2,1)}, u32[]{:S(2)}) copy-start(bf16[1,256,4096]{2,1,0:T(8,128)(2,1)} %all-gather.12.cloned.1.call-done) | copy-start | bytes 6291460
  386.7 84.4 %reduce-scatter.6.cloned.1.call-start = ((), (), s32[]{:S(2)}) async-start(), calls=%async_computation.4 | async-start | bytes 1572864 | tf_op jit(solution)/shard_map/reduce_scatter | solution.py:147
  389.4 103.2 %reduce-scatter.8.cloned.1.call-start = ((), (), s32[]{:S(2)}) async-start(), calls=%async_computation.6 | async-start | bytes 1572864 | tf_op jit(solution)/shard_map/reduce_scatter | solution.py:150
  392.3 16.5 %copy-start.5 = (bf16[1,256,512]{2,1,0:T(8,128)(2,1)S(1)}, bf16[1,256,512]{2,1,0:T(8,128)(2,1)}, u32[]{:S(2)}) copy-start(bf16[1,256,512]{2,1,0:T(8,128)(2,1)} %param.9) | copy-start | bytes 786436
  394.4 24.7 %collective-permute-start.6 = (bf16[256,512]{1,0:T(8,128)(2,1)S(1)}, bf16[256,512]{1,0:T(8,128)(2,1)S(1)}, u32[]{:S(2)}, u32[]{:S(2)}) collective-permute-start(bf16[256,512]{1,0:T(8,128)(2,1)S(1)} %get-tuple-element.16), channel_id=1, source_target_pairs={{16,0},{32,16},{48,32},{64,48},{80,64},{96,80},{112,96},{128,112},... | collective-permute-start | bytes 786440 | tf_op jit(solution)/shard_map/ppermute | solution.py:17
  409.8 41.7 %collective-permute-start = (bf16[256,512]{1,0:T(8,128)(2,1)S(1)}, bf16[256,512]{1,0:T(8,128)(2,1)S(1)}, u32[]{:S(2)}, u32[]{:S(2)}) collective-permute-start(bf16[256,512]{1,0:T(8,128)(2,1)S(1)} %fusion.30), channel_id=1, source_target_pairs={{0,16},{16,32},{32,48},{48,64},{64,80},{80,96},{96,112},{112,128},... | collective-permute-start | bytes 786440 | tf_op jit(solution)/shard_map/ppermute | solution.py:17
Sparse Core Ops, SparseCore 0:
  43.9 18.6 all-gather.7
  100.1 90.4 all-reduce.10
  192.7 23.2 all-gather.9
  218.0 41.8 all-gather.11
  265.2 86.0 all-reduce.8
  357.8 50.9 reduce-scatter.3
  412.5 37.1 all-reduce.6
  453.1 17.9 reduce-scatter.5
  474.6 17.9 reduce-scatter.7
where the time goes:
time: 502 us; the launch traced here: 501 us
  waiting for transfers between devices  361 us (72%)
  blocking collectives  47 us (9%)
  starting transfers between devices  38.5 us (8%)
  matrix products  25.7 us (5%)
  between operations  15.5 us (3%)
  other arithmetic  7.09 us (1%)
  local copies, waits for them, and re-layouts  6.06 us (1%)
    psum x2, waiting for transfers between devices, prepare(): lax.psum(keyval_part.astype(jnp.bfloat16), 'tensor').astype(jnp.float32)  170 us
    all_gather x1, waiting for transfers between devices, local(): grad_full = lax.all_gather(grad, 'tensor', axis=1, tiled=True)  43.8 us
    ppermute x5, waiting for transfers between devices, partner(): return lax.ppermute(block, axis, route)  37.8 us
    ppermute x5, starting transfers between devices, partner(): return lax.ppermute(block, axis, route)  35.5 us
    psum x1, waiting for transfers between devices, local(): lax.psum(grad_wkv.astype(jnp.bfloat16), 'dp').astype(jnp.float32)  30.6 us
    all_gather x1, blocking collectives, local(): lax.all_gather(grad_q.astype(jnp.bfloat16), 'tensor', axis=1, tiled=True)  25.8 us
    all_gather x1, waiting for transfers between devices, local(): lax.all_gather(w_out[0], 'dp', axis=1, tiled=True)  23 us
    reduce_scatter x1, waiting for transfers between devices, local(): lax.psum_scatter(grad_wout.astype(jnp.bfloat16), 'dp', scatter_dimension=...  21.6 us
  transfers between devices with their start and end apart: 16, of which 13 were waited for; matrix products, arithmetic and copies ran while one was open for 4% of the time, Pallas kernels for 0%

commit v1 on v0

v1 whole, which is shorter than its diff:
```python
import functools
import math

import jax
import jax.numpy as jnp
from jax import lax
from jax.experimental import pallas as pl
from jax.experimental.pallas import tpu as pltpu
from jax.sharding import PartitionSpec as P

HEAD = 128
MESH = pl.DeviceIdType.MESH
eps = 1e-05
BF = jnp.bfloat16
F32 = jnp.float32


def mm(a, b):
    return lax.dot_general(a, b, (((1,), (0,)), ((), ())), preferred_element_type=F32)


def mm_bt(a, b):
    return lax.dot_general(a, b, (((1,), (1,)), ((), ())), preferred_element_type=F32)


def mm_at(a, b):
    return lax.dot_general(a, b, (((0,), (0,)), ((), ())), preferred_element_type=F32)


def drain(ref, sem):
    pltpu.make_async_copy(ref, ref, sem).wait()


def side_by_side(ref, first, count):
    return jnp.concatenate([ref[first + i] for i in range(count)], axis=1)


def softmax_parts(q, kc, ko, live):
    rows, span = q.shape[0], kc.shape[0]
    factor = 1.0 / math.sqrt(HEAD)
    sc = mm_bt(q, kc) * factor
    so = mm_bt(q, ko) * factor
    col = lax.broadcasted_iota(jnp.int32, sc.shape, 1)
    sc = jnp.where(col >= span - live, sc, -1e30)
    col = lax.broadcasted_iota(jnp.int32, so.shape, 1)
    line = lax.broadcasted_iota(jnp.int32, so.shape, 0)
    so = jnp.where(col <= line, so, -1e30)
    top = jnp.maximum(jnp.max(sc, axis=1, keepdims=True), jnp.max(so, axis=1, keepdims=True))
    ec, eo = jnp.exp(sc - top), jnp.exp(so - top)
    total = jnp.sum(ec, axis=1, keepdims=True) + jnp.sum(eo, axis=1, keepdims=True)
    inverse = 1.0 / total
    return ec * inverse, eo * inverse


def kernel(
    n_pipe,
    width,
    pos, gain_ref, x_hbm, parked_hbm, grad_hbm, cache_hbm, wq_hbm, wkv_hbm, wo_hbm,
    next_out, prev_out, gwq_out, gwkv_out, gwo_out, gain_out,
    x, saved, gr, cache, wq, wkv, wot,
    qs_f, qr_f, qs_b, qr_b, ks_f, kr_f, ks_b, kr_b, ss_f, sr_f, ss_b, sr_b,
    kv_f, kv_b, scale_f, scale_b, gms, gmr, mix_f, mixb_own, mixb,
    gks, gkr, gkv, gq, gq_sib, gkv_sib, nb, nb_sib,
    y, gx, zero, wog, gwq, gwkv, gn, gn_sib,
    local_sem, wot_sem, sem_s, sem_r,
):
    s, t, d = lax.axis_index("pipe"), lax.axis_index("tensor"), lax.axis_index("dp")
    sib = 1 - d
    home = t // 4
    nt = 8
    rows = x.shape[0]
    sub = rows // nt

    barrier = pltpu.get_barrier_semaphore()
    for k in range(1, nt):
        other = lax.rem(t + k, nt)
        pl.semaphore_signal(barrier, inc=1, device_id={"tensor": other}, device_id_type=MESH)
        pl.semaphore_signal(
            barrier, inc=1, device_id={"tensor": other, "dp": sib}, device_id_type=MESH
        )
    pl.semaphore_signal(barrier, inc=1, device_id={"dp": sib}, device_id_type=MESH)
    mirror = n_pipe - 1 - s
    for stage in (mirror, lax.rem(s + 1, n_pipe), lax.rem(s + n_pipe - 1, n_pipe)):
        pl.semaphore_signal(barrier, inc=1, device_id={"pipe": stage}, device_id_type=MESH)

    loads = [
        pltpu.make_async_copy(x_hbm, x, local_sem.at[0]),
        pltpu.make_async_copy(wq_hbm, wq.at[d], local_sem.at[1]),
        pltpu.make_async_copy(wkv_hbm, wkv, local_sem.at[2]),
        pltpu.make_async_copy(grad_hbm, gr.at[d], local_sem.at[3]),
        pltpu.make_async_copy(cache_hbm, cache, local_sem.at[4]),
    ]
    for load in loads:
        load.start()
    gain = gain_ref[...].astype(F32)
    zero[...] = jnp.zeros_like(zero)

    pl.semaphore_wait(barrier, 2 * (nt - 1) + 1 + 3)

    def send(src, dst, index, device, rsem=None):
        copy = pltpu.make_async_remote_copy(
            src_ref=src,
            dst_ref=dst,
            send_sem=sem_s.at[index],
            recv_sem=sem_r.at[index] if rsem is None else rsem,
            device_id=device,
            device_id_type=MESH,
        )
        copy.start()

    def got(ref, index):
        drain(ref, sem_r.at[index])

    def sent(ref, index):
        drain(ref, sem_s.at[index])

    MIRROR, WQ, WOT, GRAD, QF, KF, SF, QB, KB, SB, KVF, KVB, GM, MIXF, MIXB, GK, GKV, GQ = range(18)
    GQS, GKVS, NB, GN, NEXT, PREV, WOG, FWD = range(18, 26)

    send(parked_hbm, saved, MIRROR, {"pipe": mirror})
    send(wq_hbm, wq.at[d], WQ, {"dp": sib})
    part = wo_hbm.shape[1] // 4
    for j in range(4):
        target = 4 * d + j
        block = wo_hbm.at[:, pl.ds(j * part, part)]

        @pl.when(target != t)
        def _():
            send(block, wot.at[t], WOT, {"tensor": target}, wot_sem.at[t])

        @pl.when(target == t)
        def _():
            pltpu.make_async_copy(block, wot.at[t], wot_sem.at[t]).start()

    send(grad_hbm, gr.at[d], GRAD, {"dp": sib})

    def to_peers(src_of, dst, index):
        for k in range(1, nt):
            other = lax.rem(t + k, nt)
            send(src_of(other), dst.at[t], index, {"tensor": other})

    def project(data, qs, qr, ks, kr, ss, sr, first):
        xf = data.astype(F32)
        xg = (xf * gain).astype(BF)
        for half in range(2):
            value = mm(xg, wq[half])
            for i in range(4):
                qs[4 * half + i] = value[:, i * HEAD : (i + 1) * HEAD].astype(BF)
        value = mm(xg, wkv[...]).astype(BF)
        for i in range(nt):
            ks[i] = value[i * sub : (i + 1) * sub]
        to_peers(lambda o: qs.at[o], qr, first)
        to_peers(lambda o: ks.at[o], kr, first + 1)
        sq = xf * xf
        quarter = sq[:, :HEAD]
        for i in range(1, sq.shape[1] // HEAD):
            quarter = quarter + sq[:, i * HEAD : (i + 1) * HEAD]
        row = jnp.sum(quarter.T, axis=0, keepdims=True)
        ss[...] = jnp.broadcast_to(row, ss.shape)
        to_peers(lambda o: ss, sr, first + 2)
        qr[t] = qs[t]
        kr[t] = ks[t]
        sr[t] = ss[...]

    def combine(qr, kr, sr, kv, scale, first, kv_index):
        got(sr.at[pl.ds(0, nt - 1)], first + 2)
        row = sr[0][0:1]
        for i in range(1, nt):
            row = row + sr[i][0:1]
        row = lax.rsqrt(row / width + eps)
        scale[...] = jnp.broadcast_to(row, (HEAD, rows)).T
        got(kr.at[pl.ds(0, nt - 1)], first + 1)
        mine = kr[0].astype(F32)
        for i in range(1, nt):
            mine = mine + kr[i].astype(F32)
        part_scale = scale[pl.ds(pl.multiple_of(t * sub, sub), sub), :]
        kv[t] = (mine * jnp.concatenate([part_scale, part_scale], axis=1)).astype(BF)
        to_peers(lambda o: kv.at[t], kv, kv_index)
        got(qr.at[pl.ds(0, nt - 1)], first)
        q = qr[0].astype(F32)
        for i in range(1, nt):
            q = q + qr[i].astype(F32)
        return (q * scale[...]).astype(BF)

    loads[0].wait()
    loads[1].wait()
    loads[2].wait()
    got(wq.at[0], WQ)
    project(x[...], qs_f, qr_f, ks_f, kr_f, ss_f, sr_f, QF)

    got(saved, MIRROR)
    project(saved[...], qs_b, qr_b, ks_b, kr_b, ss_b, sr_b, QB)

    loads[3].wait()
    for h in range(nt):
        drain(wot.at[h], wot_sem.at[h])

        @pl.when(home == d)
        def _():
            send(wot.at[h], wot.at[h], FWD, {"dp": sib}, wot_sem.at[h])

    grad = gr[d]
    for h in range(nt):
        gms[h] = mm_bt(grad, wot[h]).astype(BF)
    to_peers(lambda o: gms.at[o], gmr, GM)
    gmr[t] = gms[t]

    q_f = combine(qr_f, kr_f, sr_f, kv_f, scale_f, QF, KVF)
    q_b = combine(qr_b, kr_b, sr_b, kv_b, scale_b, QB, KVB)

    loads[4].wait()
    got(kv_f.at[pl.ds(0, nt - 1)], KVF)
    span = cache.shape[1]
    own = kv_f[...].reshape(rows, 2 * HEAD)
    live = jnp.minimum(pos[0], span)
    wc, wo_ = softmax_parts(q_f, cache[0, :, :HEAD], own[:, :HEAD], live)
    mixed = mm(wc.astype(BF), cache[0, :, HEAD:]) + mm(wo_.astype(BF), own[:, HEAD:])
    mix_f[t] = mixed.astype(BF)
    to_peers(lambda o: mix_f.at[t], mix_f, MIXF)

    got(kv_b.at[pl.ds(0, nt - 1)], KVB)
    own = kv_b[...].reshape(rows, 2 * HEAD)
    live = jnp.minimum(pos[1], span)
    kc, vc, ko, vo = cache[1, :, :HEAD], cache[1, :, HEAD:], own[:, :HEAD], own[:, HEAD:]
    wc, wo_ = softmax_parts(q_b, kc, ko, live)
    pc, po = wc.astype(BF), wo_.astype(BF)
    mixb_own[...] = (mm(pc, vc) + mm(po, vo)).astype(BF)
    seat = lax.rem(t, 4)
    for k in range(nt):
        other = lax.rem(t + k, nt)
        if k == 0:

            @pl.when(home != d)
            def _():
                send(mixb_own, mixb.at[d, seat], MIXB, {"dp": sib})

            @pl.when(home == d)
            def _():
                pltpu.make_async_copy(mixb_own, mixb.at[d, seat], sem_r.at[MIXB]).start()

        else:
            send(mixb_own, mixb.at[d, seat], MIXB, {"tensor": other, "dp": home})

    got(gmr.at[pl.ds(0, nt - 1)], GM)
    gm = gmr[0].astype(F32)
    for i in range(1, nt):
        gm = gm + gmr[i].astype(F32)
    gm = gm.astype(BF)
    gpc, gpo = mm_bt(gm, vc), mm_bt(gm, vo)
    mean = jnp.sum(gpc * wc, axis=1, keepdims=True) + jnp.sum(gpo * wo_, axis=1, keepdims=True)
    factor = 1.0 / math.sqrt(HEAD)
    gsc = (wc * (gpc - mean) * factor).astype(BF)
    gso = (wo_ * (gpo - mean) * factor).astype(BF)
    gkeys = mm_at(gso, q_b).astype(BF)
    gvals = mm_at(po, gm).astype(BF)
    for i in range(nt):
        gks[i, :, :HEAD] = gkeys[i * sub : (i + 1) * sub]
        gks[i, :, HEAD:] = gvals[i * sub : (i + 1) * sub]
    to_peers(lambda o: gks.at[o], gkr, GK)
    gkr[t] = gks[t]
    gq[t] = (mm(gsc, kc) + mm(gso, ko)).astype(BF)
    to_peers(lambda o: gq.at[t], gq, GQ)

    saved_f = saved[...].astype(F32)
    wide = jnp.concatenate([scale_b[...]] * (saved.shape[1] // HEAD), axis=1)
    nb[...] = (saved_f * wide * gain).astype(BF)
    send(nb, nb_sib, NB, {"dp": sib})

    got(gkr.at[pl.ds(0, nt - 1)], GK)
    mine = gkr[0].astype(F32)
    for i in range(1, nt):
        mine = mine + gkr[i].astype(F32)
    gkv[t] = mine.astype(BF)
    to_peers(lambda o: gkv.at[t], gkv, GKV)

    got(mix_f.at[pl.ds(0, nt - 1)], MIXF)
    added = mm(side_by_side(mix_f, 0, nt), wot[...].reshape(nt * HEAD, part))
    y[...] = (x[...].astype(F32) + added).astype(BF)

    @pl.when(s < n_pipe - 1)
    def _():
        send(y, next_out, NEXT, {"pipe": s + 1})

    @pl.when(s == 0)
    def _():
        pltpu.make_async_copy(zero, next_out, sem_r.at[NEXT]).start()

    got(gr.at[0], GRAD)
    got(mixb, MIXB)
    for_out = mm_at(side_by_side(mixb.at[0], 0, 4), gr[0]) + mm_at(
        side_by_side(mixb.at[1], 0, 4), gr[1]
    )
    columns = pl.ds(pl.multiple_of(seat * part, part), part)
    for i in range(4):
        wog[i] = for_out[i * HEAD : (i + 1) * HEAD].astype(BF)
        target = 4 * d + i
        self_too = jnp.logical_and(target == t, home == d)

        @pl.when(jnp.logical_not(self_too))
        def _():
            send(wog.at[i], gwo_out.at[:, columns], WOG, {"tensor": target, "dp": home})

        @pl.when(self_too)
        def _():
            pltpu.make_async_copy(wog.at[i], gwo_out.at[:, columns], sem_r.at[WOG]).start()

    got(gq.at[pl.ds(0, nt - 1)], GQ)
    send(gq.at[pl.ds(4 * sib, 4)], gq_sib, GQS, {"dp": sib})
    got(gkv.at[pl.ds(0, nt - 1)], GKV)
    send(gkv, gkv_sib, GKVS, {"dp": sib})
    gkv_all = gkv[...].reshape(rows, 2 * HEAD)
    gnorm = mm_bt(side_by_side(gq, 0, 4), wq[0]) + mm_bt(side_by_side(gq, 4, 4), wq[1])
    gnorm = gnorm + mm_bt(gkv_all, wkv[...])
    scaled = gnorm * wide
    gx[...] = (gr[d].astype(F32) + scaled * gain).astype(BF)

    @pl.when(s > 0)
    def _():
        send(gx, prev_out, PREV, {"pipe": s - 1})

    @pl.when(s == n_pipe - 1)
    def _():
        pltpu.make_async_copy(zero, prev_out, sem_r.at[PREV]).start()

    gn[...] = jnp.broadcast_to(jnp.sum(scaled * saved_f, axis=0, keepdims=True), gn.shape)
    send(gn, gn_sib, GN, {"dp": sib})

    got(nb_sib, NB)
    got(gkv_sib, GKVS)
    gwkv[...] = mm_at(nb[...], gkv_all) + mm_at(nb_sib[...], gkv_sib[...].reshape(rows, 2 * HEAD))
    out_kv = pltpu.make_async_copy(gwkv, gwkv_out, local_sem.at[5])
    out_kv.start()
    got(gq_sib, GQS)
    mine = jnp.concatenate([gq[4 * d + i] for i in range(4)], axis=1)
    gwq[...] = (mm_at(nb[...], mine) + mm_at(nb_sib[...], side_by_side(gq_sib, 0, 4))).astype(BF)
    out_q = pltpu.make_async_copy(gwq, gwq_out, local_sem.at[6])
    out_q.start()
    got(gn_sib, GN)
    gain_out[...] = gn[0:1] + gn_sib[0:1]

    sent(saved, MIRROR)
    sent(wq.at[0], WQ)
    for j in range(4):

        @pl.when(4 * d + j != t)
        def _():
            sent(wot.at[0], WOT)

    @pl.when(home == d)
    def _():
        sent(wot, FWD)

    sent(gr.at[0], GRAD)
    seven = pl.ds(0, nt - 1)
    for ref, index in (
        (qs_f, QF), (qs_b, QB), (ks_f, KF), (ks_b, KB), (sr_f, SF), (sr_b, SB), (kv_f, KVF),
        (kv_b, KVB), (gms, GM), (mix_f, MIXF), (gks, GK), (gkv, GKV), (gq, GQ), (gq, MIXB),
    ):
        sent(ref.at[seven], index)

    @pl.when(home != d)
    def _():
        sent(mixb_own, MIXB)

    sent(gq_sib, GQS)
    sent(gkv_sib, GKVS)
    sent(nb, NB)
    sent(gn, GN)

    @pl.when(s < n_pipe - 1)
    def _():
        sent(y, NEXT)

    @pl.when(s > 0)
    def _():
        sent(gx, PREV)

    for i in range(4):

        @pl.when(jnp.logical_not(jnp.logical_and(4 * d + i == t, home == d)))
        def _():
            sent(wog.at[i], WOG)

    got(gwo_out, WOG)
    got(next_out, NEXT)
    got(prev_out, PREV)
    out_kv.wait()
    out_q.wait()


def local(fwd_in, parked, grad_in, positions, kv_cache, w_query, w_keyval, w_out, gain):
    n_pipe = lax.axis_size("pipe")
    nt = lax.axis_size("tensor")
    rows, feat = fwd_in.shape[1:]
    span = kv_cache.shape[3]
    sub = rows // nt
    part = w_out.shape[2] // 4
    any_ = pl.BlockSpec(memory_space=pl.ANY)
    vmem = pl.BlockSpec(memory_space=pltpu.VMEM)

    def V(*shape, dtype=BF):
        return pltpu.VMEM(shape, dtype)

    heads = (nt, rows, HEAD)
    strips = (nt, sub, 2 * HEAD)
    sums = (nt, 8, rows)
    out = pl.pallas_call(
        functools.partial(kernel, n_pipe, feat * nt),
        out_shape=(
            jax.ShapeDtypeStruct((rows, feat), BF),
            jax.ShapeDtypeStruct((rows, feat), BF),
            jax.ShapeDtypeStruct(w_query.shape[1:], BF),
            jax.ShapeDtypeStruct(w_keyval.shape[1:], F32),
            jax.ShapeDtypeStruct(w_out.shape[1:], BF),
            jax.ShapeDtypeStruct((1, feat), F32),
        ),
        in_specs=[pl.BlockSpec(memory_space=pltpu.SMEM), vmem] + [any_] * 7,
        out_specs=(any_,) * 5 + (vmem,),
        scratch_shapes=[
            V(rows, feat), V(rows, feat), V(2, rows, feat), V(2, span, 2 * HEAD),
            V(2, *w_query.shape[1:]), V(*w_keyval.shape[1:]), V(nt, HEAD, part),
            V(*heads), V(*heads), V(*heads), V(*heads),
            V(*strips), V(*strips), V(*strips), V(*strips),
            V(8, rows, dtype=F32), V(*sums, dtype=F32), V(8, rows, dtype=F32), V(*sums, dtype=F32),
            V(*strips), V(*strips), V(rows, HEAD, dtype=F32), V(rows, HEAD, dtype=F32),
            V(*heads), V(*heads), V(*heads), V(rows, HEAD), V(2, 4, rows, HEAD),
            V(*strips), V(*strips), V(*strips), V(*heads), V(4, rows, HEAD), V(*strips),
            V(rows, feat), V(rows, feat),
            V(rows, feat), V(rows, feat), V(rows, feat), V(4, HEAD, part),
            V(*w_query.shape[1:]), V(*w_keyval.shape[1:], dtype=F32),
            V(8, feat, dtype=F32), V(8, feat, dtype=F32),
            pltpu.SemaphoreType.DMA((7,)),
            pltpu.SemaphoreType.DMA((8,)),
            pltpu.SemaphoreType.DMA((26,)),
            pltpu.SemaphoreType.DMA((26,)),
        ],
        compiler_params=pltpu.CompilerParams(
            collective_id=0, has_side_effects=True, vmem_limit_bytes=50 * 1024 * 1024
        ),
        name="relay",
    )(
        positions.reshape(2), gain, fwd_in[0], parked[0], grad_in[0], kv_cache[0, 0],
        w_query[0], w_keyval[0], w_out[0],
    )
    next_act, prev_grad, gwq, gwkv, gwo, ggain = out
    return next_act[None], prev_grad[None], gwq[None], gwkv[None], gwo[None], ggain


def solution(mesh):
    return jax.shard_map(
        local,
        mesh=mesh,
        in_specs=(
            P("pipe", "dp", "tensor"),
            P("pipe", "dp", "tensor"),
            P("pipe", "dp", "tensor"),
            P("pipe", "dp", None),
            P("pipe", "dp", None, None, None),
            P("pipe", "tensor", "dp"),
            P("pipe", "tensor", None),
            P("pipe", "tensor", "dp"),
            P("pipe", "tensor"),
        ),
        out_specs=(
            P("pipe", "dp", "tensor"),
            P("pipe", "dp", "tensor"),
            P("pipe", "tensor", "dp"),
            P("pipe", "tensor", None),
            P("pipe", "tensor", "dp"),
            P("pipe", "tensor"),
        ),
        check_vma=False,
    )
```

time: 502 us -> 98.4 us (0.20)
  the two profiles are of different devices: /device:TPU:1 before, /device:TPU:30 now
where the time goes in v1:
time: 98.4 us; the launch traced here: 98.1 us
  Pallas kernels  87.6 us (89%)
  local copies, waits for them, and re-layouts  9.87 us (10%)
    pallas_call x1, Pallas kernels, local(): pl.pallas_call(functools.partial(kernel, n_pipe, feat * nt), out_shape=(j...  87.6 us
    unnamed x20, local copies, waits for them, and re-layouts  9.87 us

profile of v1, /device:TPU:30, one launch (start us, length us, event | category | flops | bytes accessed | tf_op | source)
XLA Modules:
  0.0 98.1 jit_solution(17189995520134406887)
XLA Ops:
  0.6 0.0 copy-start.5
  0.6 0.0 copy-start.6
  0.7 0.7 copy-done.5
  1.3 0.0 copy-done.6
  1.3 0.0 copy-start
  1.3 1.0 %copy-done = bf16[1,1,2,512,256]{4,3,2,1,0:T(8,128)(2,1)S(1)} copy-done((bf16[1,1,2,512,256]{4,3,2,1,0:T(8,128)(2,1)S(1)}, bf16[1,1,2,512,256]{4,3,2,1,0:T(8,128)(2,1)}, u32[]{:S(2)}) %copy-start) | copy-done | bytes 524312
  2.4 0.0 copy-start.1
  2.4 0.9 copy-done.1
  3.3 0.0 copy-start.2
  3.3 0.9 copy-done.2
  4.3 0.0 copy-start.3
  4.3 0.9 copy-done.3
  5.2 0.0 copy-start.4
  5.2 0.9 copy-done.4
  6.2 87.6 %relay.1 = (bf16[256,512]{1,0:T(8,128)(2,1)S(1)}, bf16[256,512]{1,0:T(8,128)(2,1)S(1)}, bf16[512,512]{1,0:T(8,128)(2,1)S(1)}, f32[512,256]{1,0:T(8,128)S(1)}, bf...) custom-call(s32[2]{0:T(128)S(1)} %bitcast.23, bf16[1,512]{1,0:T(2,128)(2,1)S(1)} %copy-done.5, ...), custom_call_target="tpu_custom_call" | custom-call | tf_op jit(solution)/shard_map/relay/pallas_call | solution.py:407
  93.8 0.7 copy.21
  94.5 0.7 copy.22
  95.2 0.8 copy.23
  96.0 0.8 copy.24
  96.8 0.8 copy.25
  97.5 0.6 copy.26
Async XLA Ops:
  0.6 0.7 copy-start.5
  0.6 0.7 copy-start.6
  1.3 1.0 %copy-start = (bf16[1,1,2,512,256]{4,3,2,1,0:T(8,128)(2,1)S(1)}, bf16[1,1,2,512,256]{4,3,2,1,0:T(8,128)(2,1)}, u32[]{:S(2)}) copy-start(bf16[1,1,2,512,256]{4,3,2,1,0:T(8,128)(2,1)} %param.13) | copy-start | bytes 1572868
  2.4 0.9 copy-start.1
  3.3 0.9 copy-start.2
  4.3 0.9 copy-start.3
  5.2 0.9 copy-start.4

commit v2 on v1

v2 whole, which is shorter than its diff:
```python
import functools
import math

import jax
import jax.numpy as jnp
from jax import lax
from jax.experimental import pallas as pl
from jax.experimental.pallas import tpu as pltpu
from jax.sharding import PartitionSpec as P

HEAD = 128
MESH = pl.DeviceIdType.MESH
eps = 1e-05
BF = jnp.bfloat16
F32 = jnp.float32


def mm(a, b):
    return lax.dot_general(a, b, (((1,), (0,)), ((), ())), preferred_element_type=F32)


def mm_bt(a, b):
    return lax.dot_general(a, b, (((1,), (1,)), ((), ())), preferred_element_type=F32)


def mm_at(a, b):
    return lax.dot_general(a, b, (((0,), (0,)), ((), ())), preferred_element_type=F32)


def drain(ref, sem):
    pltpu.make_async_copy(ref, ref, sem).wait()


def side_by_side(ref, first, count):
    return jnp.concatenate([ref[first + i] for i in range(count)], axis=1)


def softmax_parts(q, kc, ko, live):
    rows, span = q.shape[0], kc.shape[0]
    factor = 1.0 / math.sqrt(HEAD)
    sc = mm_bt(q, kc) * factor
    so = mm_bt(q, ko) * factor
    col = lax.broadcasted_iota(jnp.int32, sc.shape, 1)
    sc = jnp.where(col >= span - live, sc, -1e30)
    col = lax.broadcasted_iota(jnp.int32, so.shape, 1)
    line = lax.broadcasted_iota(jnp.int32, so.shape, 0)
    so = jnp.where(col <= line, so, -1e30)
    top = jnp.maximum(jnp.max(sc, axis=1, keepdims=True), jnp.max(so, axis=1, keepdims=True))
    ec, eo = jnp.exp(sc - top), jnp.exp(so - top)
    total = jnp.sum(ec, axis=1, keepdims=True) + jnp.sum(eo, axis=1, keepdims=True)
    inverse = 1.0 / total
    return ec * inverse, eo * inverse


def kernel(
    n_pipe,
    width,
    pos_hbm, gain_hbm, x_hbm, parked_hbm, grad_hbm, cache_hbm, wq_hbm, wkv_hbm, wo_hbm,
    next_out, prev_out, gwq_out, gwkv_out, gwo_out, gain_out,
    x, saved, gr, cache, wq, wkv, wot,
    qs_f, qr_f, qs_b, qr_b, ks_f, kr_f, ks_b, kr_b, ss_f, sr_f, ss_b, sr_b,
    kv_f, kv_b, scale_f, scale_b, gms, gmr, mix_f, mixb_own, mixb,
    gks, gkr, gkv, gq, gq_sib, gkv_sib, nb, nb_sib,
    y, gx, zero, wog, gn, gn_sib,
    pos, gain_ref, local_sem, wot_sem, sem_s, sem_r,
):
    s, t, d = lax.axis_index("pipe"), lax.axis_index("tensor"), lax.axis_index("dp")
    sib = 1 - d
    home = t // 4
    nt = 8
    rows = x.shape[0]
    parts_b = qs_b.shape[0]

    barrier = pltpu.get_barrier_semaphore()
    mirror = n_pipe - 1 - s
    for stage in (mirror, lax.rem(s + 1, n_pipe), lax.rem(s + n_pipe - 1, n_pipe)):
        pl.semaphore_signal(barrier, inc=1, device_id={"pipe": stage}, device_id_type=MESH)
    for k in range(1, nt):
        other = lax.rem(t + k, nt)
        pl.semaphore_signal(barrier, inc=1, device_id={"tensor": other}, device_id_type=MESH)
        pl.semaphore_signal(
            barrier, inc=1, device_id={"tensor": other, "dp": sib}, device_id_type=MESH
        )
    pl.semaphore_signal(barrier, inc=1, device_id={"dp": sib}, device_id_type=MESH)

    loads = [
        pltpu.make_async_copy(x_hbm, x, local_sem.at[0]),
        pltpu.make_async_copy(wkv_hbm, wkv, local_sem.at[2]),
        pltpu.make_async_copy(wq_hbm, wq.at[d], local_sem.at[1]),
        pltpu.make_async_copy(grad_hbm, gr.at[d], local_sem.at[3]),
        pltpu.make_async_copy(cache_hbm, cache, local_sem.at[4]),
        pltpu.make_async_copy(gain_hbm, gain_ref, local_sem.at[5]),
        pltpu.make_async_copy(pos_hbm, pos, local_sem.at[6]),
    ]
    for load in loads:
        load.start()
    zero[...] = jnp.zeros_like(zero)

    pl.semaphore_wait(barrier, 2 * (nt - 1) + 1 + 3)

    names = (
        "WQ", "WOT", "FWD", "GRAD", "QF", "KF", "SF", "KVF", "GM", "MIXF", "MIXB", "GK", "GKV", "GQ",
        "GQS", "GKVS", "NB", "GN", "NEXT", "PREV", "WOG",
    )
    at = {name: i for i, name in enumerate(names)}
    index_of = len(names)
    for name in ("MIRROR", "QB", "KB", "SB", "KVB"):
        for c in range(parts_b):
            at[name, c] = index_of
            index_of += 1

    def send(src, dst, name, device, rsem=None):
        pltpu.make_async_remote_copy(
            src_ref=src,
            dst_ref=dst,
            send_sem=sem_s.at[at[name]],
            recv_sem=sem_r.at[at[name]] if rsem is None else rsem,
            device_id=device,
            device_id_type=MESH,
        ).start()

    def got(ref, name):
        drain(ref, sem_r.at[at[name]])

    def sent(ref, name):
        drain(ref, sem_s.at[at[name]])

    def to_peers(src_of, dst, name):
        for k in range(1, nt):
            other = lax.rem(t + k, nt)
            send(src_of(other), dst.at[t], name, {"tensor": other})

    seven = pl.ds(0, nt - 1)

    chunk = rows // parts_b
    for c in range(parts_b):
        cut = pl.ds(c * chunk, chunk)
        send(parked_hbm.at[cut], saved.at[cut], ("MIRROR", c), {"pipe": mirror})
    send(wq_hbm, wq.at[d], "WQ", {"dp": sib})
    part = wo_hbm.shape[1] // 4
    for j in range(4):
        target = 4 * d + j
        block = wo_hbm.at[:, pl.ds(j * part, part)]

        @pl.when(target != t)
        def _():
            send(block, wot.at[t], "WOT", {"tensor": target}, wot_sem.at[t])

        @pl.when(target == t)
        def _():
            pltpu.make_async_copy(block, wot.at[t], wot_sem.at[t]).start()

    def project(data, qs, qr, ks, kr, ss, sr, names, ready=None):
        sub = ks.shape[1]
        xf = data.astype(F32)
        xg = (xf * gain).astype(BF)
        value = mm(xg, wkv[...]).astype(BF)
        for i in range(nt):
            ks[i] = value[i * sub : (i + 1) * sub]
        to_peers(lambda o: ks.at[o], kr, names[1])
        sq = xf * xf
        quarter = sq[:, :HEAD]
        for i in range(1, sq.shape[1] // HEAD):
            quarter = quarter + sq[:, i * HEAD : (i + 1) * HEAD]
        row = jnp.sum(quarter.T, axis=0, keepdims=True)
        ss[...] = jnp.broadcast_to(row, ss.shape)
        to_peers(lambda o: ss, sr, names[2])
        if ready is not None:
            ready()
        for half in range(2):
            value = mm(xg, wq[half])
            for i in range(4):
                qs[4 * half + i] = value[:, i * HEAD : (i + 1) * HEAD].astype(BF)
        to_peers(lambda o: qs.at[o], qr, names[0])
        qr[t] = qs[t]
        kr[t] = ks[t]
        sr[t] = ss[...]

    def combine_keyval(kr, sr, kv, scale, names):
        sub = kr.shape[1]
        got(sr.at[seven], names[2])
        totals = sr[0]
        for i in range(1, nt):
            totals = totals + sr[i]
        row = lax.rsqrt(totals / width + eps)[0:1]
        scale[...] = jnp.broadcast_to(row, (HEAD, row.shape[1])).T
        got(kr.at[seven], names[1])
        mine = kr[0].astype(F32)
        for i in range(1, nt):
            mine = mine + kr[i].astype(F32)
        part_scale = scale[pl.ds(pl.multiple_of(t * sub, sub), sub), :]
        kv[t] = (mine * jnp.concatenate([part_scale, part_scale], axis=1)).astype(BF)
        to_peers(lambda o: kv.at[t], kv, names[3])

    def combine_query(qr, scale, names):
        got(qr.at[seven], names[0])
        q = qr[0].astype(F32)
        for i in range(1, nt):
            q = q + qr[i].astype(F32)
        return (q * scale[...]).astype(BF)

    names_f = ("QF", "KF", "SF", "KVF")

    def ready():
        loads[2].wait()
        got(wq.at[0], "WQ")

    loads[0].wait()
    loads[1].wait()
    loads[5].wait()
    gain = gain_ref[...].astype(F32)
    project(x[...], qs_f, qr_f, ks_f, kr_f, ss_f, sr_f, names_f, ready)

    send(grad_hbm, gr.at[d], "GRAD", {"dp": sib})
    names_b = [(("QB", c), ("KB", c), ("SB", c), ("KVB", c)) for c in range(parts_b)]
    for c in range(parts_b):
        cut = pl.ds(c * chunk, chunk)
        got(saved.at[cut], ("MIRROR", c))
        project(
            saved[cut], qs_b.at[c], qr_b.at[c], ks_b.at[c], kr_b.at[c], ss_b.at[c], sr_b.at[c],
            names_b[c],
        )
        if c == 0:
            loads[3].wait()
            for h in range(nt):
                drain(wot.at[h], wot_sem.at[h])

                @pl.when(home == d)
                def _():
                    send(wot.at[h], wot.at[h], "FWD", {"dp": sib}, wot_sem.at[h])

    combine_keyval(kr_f, sr_f, kv_f, scale_f, names_f)
    grad = gr[d]
    for h in range(nt):
        gms[h] = mm_bt(grad, wot[h]).astype(BF)
    to_peers(lambda o: gms.at[o], gmr, "GM")
    gmr[t] = gms[t]

    q_f = combine_query(qr_f, scale_f, names_f)
    for c in range(parts_b):
        combine_keyval(kr_b.at[c], sr_b.at[c], kv_b.at[c], scale_b.at[c], names_b[c])

    loads[4].wait()
    loads[6].wait()
    got(kv_f.at[seven], "KVF")
    span = cache.shape[1]
    own = kv_f[...].reshape(rows, 2 * HEAD)
    live = jnp.minimum(pos[0, 0], span)
    wc, wo_ = softmax_parts(q_f, cache[0, :, :HEAD], own[:, :HEAD], live)
    mixed = mm(wc.astype(BF), cache[0, :, HEAD:]) + mm(wo_.astype(BF), own[:, HEAD:])
    mix_f[t] = mixed.astype(BF)
    to_peers(lambda o: mix_f.at[t], mix_f, "MIXF")

    q_b = jnp.concatenate(
        [combine_query(qr_b.at[c], scale_b.at[c], names_b[c]) for c in range(parts_b)], axis=0
    )
    for c in range(parts_b):
        got(kv_b.at[c, seven], ("KVB", c))
    own = kv_b[...].reshape(rows, 2 * HEAD)
    live = jnp.minimum(pos[0, 1], span)
    kc, vc, ko, vo = cache[1, :, :HEAD], cache[1, :, HEAD:], own[:, :HEAD], own[:, HEAD:]
    wc, wo_ = softmax_parts(q_b, kc, ko, live)
    pc, po = wc.astype(BF), wo_.astype(BF)

    mixb_own[...] = (mm(pc, vc) + mm(po, vo)).astype(BF)
    seat = lax.rem(t, 4)
    for k in range(nt):
        other = lax.rem(t + k, nt)
        if k == 0:

            @pl.when(home != d)
            def _():
                send(mixb_own, mixb.at[d, seat], "MIXB", {"dp": sib})

            @pl.when(home == d)
            def _():
                pltpu.make_async_copy(mixb_own, mixb.at[d, seat], sem_r.at[at["MIXB"]]).start()

        else:
            send(mixb_own, mixb.at[d, seat], "MIXB", {"tensor": other, "dp": home})


    got(gmr.at[seven], "GM")
    gm = gmr[0].astype(F32)
    for i in range(1, nt):
        gm = gm + gmr[i].astype(F32)
    gm = gm.astype(BF)
    gpc, gpo = mm_bt(gm, vc), mm_bt(gm, vo)
    mean = jnp.sum(gpc * wc, axis=1, keepdims=True) + jnp.sum(gpo * wo_, axis=1, keepdims=True)
    factor = 1.0 / math.sqrt(HEAD)
    gso = (wo_ * (gpo - mean) * factor).astype(BF)
    gkeys = mm_at(gso, q_b).astype(BF)
    gvals = mm_at(po, gm).astype(BF)
    sub = rows // nt
    for i in range(nt):
        gks[i, :, :HEAD] = gkeys[i * sub : (i + 1) * sub]
        gks[i, :, HEAD:] = gvals[i * sub : (i + 1) * sub]
    to_peers(lambda o: gks.at[o], gkr, "GK")
    gkr[t] = gks[t]
    gsc = (wc * (gpc - mean) * factor).astype(BF)
    gq[t] = (mm(gsc, kc) + mm(gso, ko)).astype(BF)
    to_peers(lambda o: gq.at[t], gq, "GQ")

    saved_f = saved[...].astype(F32)
    scale = scale_b[...].reshape(rows, HEAD)
    wide = jnp.concatenate([scale] * (saved.shape[1] // HEAD), axis=1)
    nb[...] = (saved_f * wide * gain).astype(BF)
    send(nb, nb_sib, "NB", {"dp": sib})

    got(mix_f.at[seven], "MIXF")
    added = mm(side_by_side(mix_f, 0, nt), wot[...].reshape(nt * HEAD, part))
    y[...] = (x[...].astype(F32) + added).astype(BF)

    @pl.when(s < n_pipe - 1)
    def _():
        send(y, next_out, "NEXT", {"pipe": s + 1})

    @pl.when(s == 0)
    def _():
        pltpu.make_async_copy(zero, next_out, sem_r.at[at["NEXT"]]).start()

    got(gkr.at[seven], "GK")
    mine = gkr[0].astype(F32)
    for i in range(1, nt):
        mine = mine + gkr[i].astype(F32)
    gkv[t] = mine.astype(BF)
    to_peers(lambda o: gkv.at[t], gkv, "GKV")

    got(gr.at[0], "GRAD")
    got(mixb, "MIXB")
    for_out = mm_at(side_by_side(mixb.at[0], 0, 4), gr[0]) + mm_at(
        side_by_side(mixb.at[1], 0, 4), gr[1]
    )
    columns = pl.ds(pl.multiple_of(seat * part, part), part)
    for i in range(4):
        wog[i] = for_out[i * HEAD : (i + 1) * HEAD].astype(BF)
        target = 4 * d + i
        self_too = jnp.logical_and(target == t, home == d)

        @pl.when(jnp.logical_not(self_too))
        def _():
            send(wog.at[i], gwo_out.at[:, columns], "WOG", {"tensor": target, "dp": home})

        @pl.when(self_too)
        def _():
            pltpu.make_async_copy(
                wog.at[i], gwo_out.at[:, columns], sem_r.at[at["WOG"]]
            ).start()

    got(gq.at[seven], "GQ")
    send(gq.at[pl.ds(4 * sib, 4)], gq_sib, "GQS", {"dp": sib})
    gnorm = mm_bt(side_by_side(gq, 0, 4), wq[0]) + mm_bt(side_by_side(gq, 4, 4), wq[1])
    got(gkv.at[seven], "GKV")
    send(gkv, gkv_sib, "GKVS", {"dp": sib})
    gkv_all = gkv[...].reshape(rows, 2 * HEAD)
    scaled = (gnorm + mm_bt(gkv_all, wkv[...])) * wide
    gx[...] = (gr[d].astype(F32) + scaled * gain).astype(BF)

    @pl.when(s > 0)
    def _():
        send(gx, prev_out, "PREV", {"pipe": s - 1})

    @pl.when(s == n_pipe - 1)
    def _():
        pltpu.make_async_copy(zero, prev_out, sem_r.at[at["PREV"]]).start()

    gn[...] = jnp.broadcast_to(jnp.sum(scaled * saved_f, axis=0, keepdims=True), gn.shape)
    send(gn, gn_sib, "GN", {"dp": sib})

    got(nb_sib, "NB")
    got(gkv_sib, "GKVS")
    gwkv_out[...] = mm_at(nb[...], gkv_all) + mm_at(
        nb_sib[...], gkv_sib[...].reshape(rows, 2 * HEAD)
    )
    got(gq_sib, "GQS")
    mine = jnp.concatenate([gq[4 * d + i] for i in range(4)], axis=1)
    gwq_out[...] = (
        mm_at(nb[...], mine) + mm_at(nb_sib[...], side_by_side(gq_sib, 0, 4))
    ).astype(BF)
    got(gn_sib, "GN")
    gain_out[...] = gn[0:1] + gn_sib[0:1]

    for c in range(parts_b):
        cut = pl.ds(c * chunk, chunk)
        sent(saved.at[cut], ("MIRROR", c))
        sent(qs_b.at[c, seven], ("QB", c))
        sent(ks_b.at[c, seven], ("KB", c))
        sent(sr_b.at[c, seven], ("SB", c))
        sent(kv_b.at[c, seven], ("KVB", c))
    sent(wq.at[0], "WQ")
    for j in range(4):

        @pl.when(4 * d + j != t)
        def _():
            sent(wot.at[0], "WOT")

    @pl.when(home == d)
    def _():
        sent(wot, "FWD")

    sent(gr.at[0], "GRAD")
    for ref, name in (
        (qs_f, "QF"), (ks_f, "KF"), (sr_f, "SF"), (kv_f, "KVF"), (gms, "GM"), (mix_f, "MIXF"),
        (gks, "GK"), (gkv, "GKV"), (gq, "GQ"), (gq, "MIXB"),
    ):
        sent(ref.at[seven], name)

    @pl.when(home != d)
    def _():
        sent(mixb_own, "MIXB")

    sent(gq_sib, "GQS")
    sent(gkv_sib, "GKVS")
    sent(nb, "NB")
    sent(gn, "GN")

    @pl.when(s < n_pipe - 1)
    def _():
        sent(y, "NEXT")

    @pl.when(s > 0)
    def _():
        sent(gx, "PREV")

    for i in range(4):

        @pl.when(jnp.logical_not(jnp.logical_and(4 * d + i == t, home == d)))
        def _():
            sent(wog.at[i], "WOG")

    got(gwo_out, "WOG")
    got(next_out, "NEXT")
    got(prev_out, "PREV")


def place(*refs):
    count = len(refs) // 2
    sem = refs[-1]
    copies = [
        pltpu.make_async_copy(refs[i], refs[count + i], sem.at[i]) for i in range(count)
    ]
    for copy in copies:
        copy.start()
    for copy in copies:
        copy.wait()


def local(fwd_in, parked, grad_in, positions, kv_cache, w_query, w_keyval, w_out, gain):
    n_pipe = lax.axis_size("pipe")
    nt = lax.axis_size("tensor")
    rows, feat = fwd_in.shape[1:]
    span = kv_cache.shape[3]
    part = w_out.shape[2] // 4
    any_ = pl.BlockSpec(memory_space=pltpu.HBM)
    vmem = pl.BlockSpec(memory_space=pltpu.VMEM)

    def V(*shape, dtype=BF):
        return pltpu.VMEM(shape, dtype)

    parts_b = 2
    cut = rows // parts_b
    heads = (nt, rows, HEAD)
    heads_b = (parts_b, nt, cut, HEAD)
    strips = (nt, rows // nt, 2 * HEAD)
    strips_b = (parts_b, nt, cut // nt, 2 * HEAD)

    out = pl.pallas_call(
        functools.partial(kernel, n_pipe, feat * nt),
        out_shape=(
            pltpu.VMEM((rows, feat), BF),
            pltpu.VMEM((rows, feat), BF),
            pltpu.VMEM(w_query.shape[1:], BF),
            pltpu.VMEM(w_keyval.shape[1:], F32),
            pltpu.VMEM(w_out.shape[1:], BF),
            pltpu.VMEM((1, feat), F32),
        ),
        in_specs=[any_] * 9,
        out_specs=(vmem,) * 6,
        scratch_shapes=[
            V(rows, feat), V(rows, feat), V(2, rows, feat), V(2, span, 2 * HEAD),
            V(2, *w_query.shape[1:]), V(*w_keyval.shape[1:]), V(nt, HEAD, part),
            V(*heads), V(*heads), V(*heads_b), V(*heads_b),
            V(*strips), V(*strips), V(*strips_b), V(*strips_b),
            V(8, rows, dtype=F32), V(nt, 8, rows, dtype=F32),
            V(parts_b, 8, cut, dtype=F32), V(parts_b, nt, 8, cut, dtype=F32),
            V(*strips), V(*strips_b), V(rows, HEAD, dtype=F32), V(parts_b, cut, HEAD, dtype=F32),
            V(*heads), V(*heads), V(*heads), V(rows, HEAD), V(2, 4, rows, HEAD),
            V(*strips), V(*strips), V(*strips), V(*heads), V(4, rows, HEAD), V(*strips),
            V(rows, feat), V(rows, feat),
            V(rows, feat), V(rows, feat), V(rows, feat), V(4, HEAD, part),
            V(8, feat, dtype=F32), V(8, feat, dtype=F32),
            pltpu.SMEM((1, 2), jnp.int32), V(1, feat),
            pltpu.SemaphoreType.DMA((7,)),
            pltpu.SemaphoreType.DMA((8,)),
            pltpu.SemaphoreType.DMA((22 + 5 * parts_b,)),
            pltpu.SemaphoreType.DMA((22 + 5 * parts_b,)),
        ],
        compiler_params=pltpu.CompilerParams(
            collective_id=0, has_side_effects=True, vmem_limit_bytes=32 * 1024 * 1024
        ),
        name="relay",
    )(
        *(
            pltpu.with_memory_space_constraint(v, pltpu.HBM)
            for v in (
                positions[0], gain, fwd_in[0], parked[0], grad_in[0], kv_cache[0, 0], w_query[0], w_keyval[0], w_out[0]
            )
        ),
    )
    next_act, prev_grad, gwq, gwkv, gwo, ggain = pl.pallas_call(
        place,
        out_shape=tuple(jax.ShapeDtypeStruct(v.shape, v.dtype) for v in out),
        in_specs=[vmem] * len(out),
        out_specs=(any_,) * len(out),
        scratch_shapes=[pltpu.SemaphoreType.DMA((len(out),))],
        compiler_params=pltpu.CompilerParams(vmem_limit_bytes=4 * 1024 * 1024),
        name="place",
    )(*out)
    return next_act[None], prev_grad[None], gwq[None], gwkv[None], gwo[None], ggain


def solution(mesh):
    return jax.shard_map(
        local,
        mesh=mesh,
        in_specs=(
            P("pipe", "dp", "tensor"),
            P("pipe", "dp", "tensor"),
            P("pipe", "dp", "tensor"),
            P("pipe", "dp", None),
            P("pipe", "dp", None, None, None),
            P("pipe", "tensor", "dp"),
            P("pipe", "tensor", None),
            P("pipe", "tensor", "dp"),
            P("pipe", "tensor"),
        ),
        out_specs=(
            P("pipe", "dp", "tensor"),
            P("pipe", "dp", "tensor"),
            P("pipe", "tensor", "dp"),
            P("pipe", "tensor", None),
            P("pipe", "tensor", "dp"),
            P("pipe", "tensor"),
        ),
        check_vma=False,
    )
```

time: 98.4 us -> 87 us (0.88)
  local copies, waits for them, and re-layouts: 9.87 us -> 0 us
  Pallas kernels: 87.6 us -> 86.3 us
    unnamed x20 -> x0, local copies, waits for them, and re-layouts: 9.87 us -> none
    pallas_call x1 -> x2, Pallas kernels: 87.6 us -> 86.3 us  [the longest x1 84.9 us: local(): pl.pallas_call(functools.partial(kernel, n_pipe, feat * nt), out_shape=(p...]
where the time goes in v2:
time: 87 us; the launch traced here: 86.9 us
  Pallas kernels  86.3 us (99%)
    pallas_call x1, Pallas kernels, local(): pl.pallas_call(functools.partial(kernel, n_pipe, feat * nt), out_shape=(p...  84.9 us

profile of v2, /device:TPU:30, one launch (start us, length us, event | category | flops | bytes accessed | tf_op | source)
XLA Modules:
  0.0 86.9 jit_solution(1120014542316510246)
XLA Ops:
  0.6 84.9 %relay.1 = (bf16[256,512]{1,0:T(8,128)(2,1)S(1)}, bf16[256,512]{1,0:T(8,128)(2,1)S(1)}, bf16[512,512]{1,0:T(8,128)(2,1)S(1)}, f32[512,256]{1,0:T(8,128)S(1)}, bf...) custom-call(s32[1,2]{1,0:T(1,128)} %bitcast.20, bf16[1,512]{1,0:T(2,128)(2,1)} %gain_hbm.1, bf16[256,512]{1,0:T(8,128)(2,1)} %bitcast.16, ...), custom_call_target="tpu_custom_call" | custom-call | tf_op jit(solution)/shard_map/relay/pallas_call | solution.py:467
  85.5 1.4 %place.1 = (bf16[256,512]{1,0:T(8,128)(2,1)}, bf16[256,512]{1,0:T(8,128)(2,1)}, bf16[512,512]{1,0:T(8,128)(2,1)}, f32[512,256]{1,0:T(8,128)}, bf16[128,2048]{1,0:T(8,128)(2,1)}, /*index=5*/f32[1,512]{1,0:T(1,128)}) custom-call(bf16[256,512]{1,0:T(8,128)(2,1)S(1)} %get-tuple-element.18.refs_0_, bf16[256,512]{1,0:T(8,128)(2,1)S(1)} %get-tuple-element.19.refs_1_, ...), custom_call_target="tpu_custom_call" | custom-call | tf_op jit(solution)/shard_map/place/pallas_call | solution.py:510

commit v3 on v2

--- a/solution.py
+++ b/solution.py
@@ -171,7 +171,13 @@
             value = mm(xg, wq[half])
             for i in range(4):
                 qs[4 * half + i] = value[:, i * HEAD : (i + 1) * HEAD].astype(BF)
-        to_peers(lambda o: qs.at[o], qr, names[0])
+            for i in range(4):
+                head = 4 * half + lax.rem(t + i, 4)
+
+                @pl.when(head != t)
+                def _():
+                    send(qs.at[head], qr.at[t], names[0], {"tensor": head})
+
         qr[t] = qs[t]
         kr[t] = ks[t]
         sr[t] = ss[...]
@@ -230,14 +236,16 @@
                     send(wot.at[h], wot.at[h], "FWD", {"dp": sib}, wot_sem.at[h])
 
     combine_keyval(kr_f, sr_f, kv_f, scale_f, names_f)
+    combine_keyval(kr_b.at[0], sr_b.at[0], kv_b.at[0], scale_b.at[0], names_b[0])
     grad = gr[d]
-    for h in range(nt):
-        gms[h] = mm_bt(grad, wot[h]).astype(BF)
-    to_peers(lambda o: gms.at[o], gmr, "GM")
-    gmr[t] = gms[t]
+    for k in range(1, nt):
+        other = lax.rem(t + k, nt)
+        gms[other] = mm_bt(grad, wot[other]).astype(BF)
+        send(gms.at[other], gmr.at[t], "GM", {"tensor": other})
+    gmr[t] = mm_bt(grad, wot[t]).astype(BF)
 
     q_f = combine_query(qr_f, scale_f, names_f)
-    for c in range(parts_b):
+    for c in range(1, parts_b):
         combine_keyval(kr_b.at[c], sr_b.at[c], kv_b.at[c], scale_b.at[c], names_b[c])
 
     loads[4].wait()

time: 87 us -> 88.5 us (1.017)
  the two profiles are of different devices: /device:TPU:30 before, /device:TPU:24 now
where the time goes in v3:
time: 88.5 us; the launch traced here: 88.4 us
  Pallas kernels  87.8 us (99%)
    pallas_call x1, Pallas kernels, local(): pl.pallas_call(functools.partial(kernel, n_pipe, feat * nt), out_shape=(p...  86.4 us

profile of v3, /device:TPU:24, one launch (start us, length us, event | category | flops | bytes accessed | tf_op | source)
XLA Modules:
  0.0 88.4 jit_solution(3870762711034276554)
XLA Ops:
  0.6 86.4 %relay.1 = (bf16[256,512]{1,0:T(8,128)(2,1)S(1)}, bf16[256,512]{1,0:T(8,128)(2,1)S(1)}, bf16[512,512]{1,0:T(8,128)(2,1)S(1)}, f32[512,256]{1,0:T(8,128)S(1)}, bf...) custom-call(s32[1,2]{1,0:T(1,128)} %bitcast.20, bf16[1,512]{1,0:T(2,128)(2,1)} %gain_hbm.1, bf16[256,512]{1,0:T(8,128)(2,1)} %bitcast.16, ...), custom_call_target="tpu_custom_call" | custom-call | tf_op jit(solution)/shard_map/relay/pallas_call | solution.py:475
  87.1 1.4 %place.1 = (bf16[256,512]{1,0:T(8,128)(2,1)}, bf16[256,512]{1,0:T(8,128)(2,1)}, bf16[512,512]{1,0:T(8,128)(2,1)}, f32[512,256]{1,0:T(8,128)}, bf16[128,2048]{1,0:T(8,128)(2,1)}, /*index=5*/f32[1,512]{1,0:T(1,128)}) custom-call(bf16[256,512]{1,0:T(8,128)(2,1)S(1)} %get-tuple-element.18.refs_0_, bf16[256,512]{1,0:T(8,128)(2,1)S(1)} %get-tuple-element.19.refs_1_, ...), custom_call_target="tpu_custom_call" | custom-call | tf_op jit(solution)/shard_map/place/pallas_call | solution.py:518
